TPU v7x, 128 devices: a whole 4x4x4 slice. The times are simulated.
128 devices in a mesh: ctx: 8 (over z_hi, y), tp: 16 (over z_lo, x, core).
Axes of the slice: x: 4, y: 4, z: 4 (z_hi: 2, z_lo: 2; z = z_hi * 2 + z_lo), core: 2. Of those that a mesh axis runs over, the one named last changes fastest.
Arguments:
- out_grad: bfloat16 [16384, 4096], P(('ctx', 'tp')), may hold values from -6 to 6
- combine_weights: bfloat16 [16384, 8], P(('ctx', 'tp')), may hold values from 0.029907227 to 0.3984375
- expert_ids: int32 [16384, 8], P(('ctx', 'tp')), may hold values from 0 to 127, all different within a row; in each aligned block of 128 rows (0 to 127, 128 to 255, ...) at most 10 rows name the same one
- hidden_saved: bfloat16 [128, 1280, 1536], P(('ctx', 'tp')), may hold values from -0.29882812 to 0.29882812
- down_weight: bfloat16 [128, 1536, 4096], P(('ctx', 'tp')), may hold values from -0.15625 to 0.15625
Outputs:
- hidden_grad: bfloat16 [128, 1280, 1536], P(('ctx', 'tp'))
- combine_grad: float32 [16384, 8], P(('ctx', 'tp'))
Inputs may be any that keep to these rules, and one draw needn't show every extreme that they name: `expert_ids`: the 8 ids of a token differ. Among the rows of one device no expert is named more than 10 times, a bound that some block reaches.
All inputs are finite; a program needn't handle non-finite values.
Results may differ from a plain program's by a relative error of at most 0.001.
Values may be sent and summed in bfloat16 or wider, within the bound.
A program may use at most 192 MiB of HBM per device.

v0:
```python
import jax
import jax.numpy as jnp
from jax import lax
from jax.sharding import PartitionSpec as P


def per_device(out_grad, combine_weights, expert_ids, hidden_saved, down_weight):
    ctx_count = lax.axis_size("ctx")
    tp_count = lax.axis_size("tp")
    experts_count = ctx_count * tp_count
    tok_count, top_count = expert_ids.shape
    slot_rows = hidden_saved.shape[1]
    capacity = slot_rows // experts_count
    width = out_grad.shape[1]
    routed = expert_ids.reshape(-1)
    onehot = (routed[:, None] == jnp.arange(experts_count, dtype=jnp.int32)[None, :]).astype(
        jnp.int32
    )
    position = jnp.sum(jnp.cumsum(onehot, axis=0) * onehot, axis=1) - 1
    slot_index = routed * capacity + position
    token_index = jnp.arange(tok_count * top_count, dtype=jnp.int32) // top_count
    send_grad = (
        jnp.zeros((slot_rows, width), jnp.bfloat16).at[slot_index].set(out_grad[token_index])
    )
    send_weight = (
        jnp.zeros((slot_rows,), jnp.bfloat16).at[slot_index].set(combine_weights.reshape(-1))
    )
    recv_grad, recv_weight = (
        lax.all_to_all(
            send_grad.reshape(experts_count, capacity, width),
            ("ctx", "tp"),
            split_axis=0,
            concat_axis=0,
            tiled=True,
        ),
        lax.all_to_all(
            send_weight.reshape(experts_count, capacity),
            ("ctx", "tp"),
            split_axis=0,
            concat_axis=0,
            tiled=True,
        ),
    )
    slot_grad = recv_grad.reshape(slot_rows, width)
    slot_weight = recv_weight.reshape(slot_rows, 1).astype(jnp.float32)
    raw = lax.dot_general(
        slot_grad, down_weight[0], (((1,), (1,)), ((), ())), preferred_element_type=jnp.float32
    )
    hidden_grad = (slot_weight * raw).astype(jnp.bfloat16)[None]
    slot_back = jnp.sum(hidden_saved[0].astype(jnp.float32) * raw, axis=1)
    returned = lax.all_to_all(
        slot_back.reshape(experts_count, capacity),
        ("ctx", "tp"),
        split_axis=0,
        concat_axis=0,
        tiled=True,
    )
    combine_grad = returned.reshape(-1)[slot_index].reshape(tok_count, top_count)
    return (hidden_grad, combine_grad)


def solution(mesh):
    in_specs = (
        P(("ctx", "tp"), None),
        P(("ctx", "tp"), None),
        P(("ctx", "tp"), None),
        P(("ctx", "tp"), None, None),
        P(("ctx", "tp"), None, None),
    )
    out_specs = (P(("ctx", "tp"), None, None), P(("ctx", "tp"), None))
    return jax.shard_map(
        per_device, mesh=mesh, in_specs=in_specs, out_specs=out_specs, check_vma=False
    )
```

profile of v0, /device:TPU:1, one launch (start us, length us, event | category | flops | bytes accessed | tf_op | source)
XLA Modules:
  0.0 370.8 jit_solution(13386364590012443850)
XLA Ops:
  0.6 0.9 copy.15
  1.5 0.1 eq.29
  1.6 0.1 eq.25
  1.7 0.7 broadcast_multiply_fusion
  2.4 0.1 copy.17
  2.5 0.2 fusion.7
  2.8 0.1 copy.18
  2.9 0.4 fusion.6
  3.3 0.1 copy.14
  3.4 0.1 mul.32
  3.5 0.8 copy.19
  4.3 0.1 reshape.163
  4.4 7.6 %scatter_custom_fusion = bf16[1280]{0:T(1024)(128)(2,1)S(1)} fusion(s32[1024]{0:T(1024)S(1)} %bitcast.23, bf16[1024]{0:T(1024)(128)(2,1)S(1)} %reshape.163, bf16[]{:T(256)} %constant.27.clone.1), kind=kCustom, calls=%fused_computation.32 | custom fusion | bytes 2562 | tf_op jit(solution)/shard_map/scatter | solution.py:26
  12.0 0.8 all_to_all.20
  12.8 11.5 %all-to-all-start = ((bf16[128,1,10]{2,1,0:T(2,128)(2,1)}), bf16[128,1,10]{2,1,0:T(2,128)(2,1)S(1)}, u32[]{:S(2)}, u32[]{:S(2)}) async-start(bf16[128,1,10]{2,1,0:T(2,128)(2,1)} %all_to_all.20), calls=%async_computation | async-start | bytes 131072 | tf_op jit(solution)/shard_map/all_to_all | solution.py:36
  24.3 7.8 %gather_fusion = bf16[1024,4096]{1,0:T(8,128)(2,1)} fusion(bf16[128,4096]{1,0:T(8,128)(2,1)S(1)} %copy-done, s32[1024]{0:T(1024)S(1)} %broadcast_clamp_fusion.1), kind=kCustom, calls=%fused_computation | custom fusion | bytes 16781312 | tf_op jit(solution)/shard_map/gather | solution.py:23
  32.1 18.8 %scatter_custom_fusion.1 = bf16[1280,4096]{1,0:T(8,128)(2,1)} fusion(s32[1024]{0:T(1024)S(1)} %bitcast.24, bf16[1024,4096]{1,0:T(8,128)(2,1)} %gather_fusion, bf16[]{:T(256)} %constant.27.clone.1), kind=kCustom, calls=%fused_computation.9 | custom fusion | bytes 10486272 | tf_op jit(solution)/shard_map/scatter | solution.py:23
  51.0 15.2 %reshape.137 = bf16[128,10,4096]{2,1,0:T(8,128)(2,1)} reshape(bf16[1280,4096]{1,0:T(8,128)(2,1)} %scatter_custom_fusion.1) | data formatting | bytes 20971520 | tf_op jit(solution)/shard_map/reshape | solution.py:30
  66.2 10.2 %all-to-all-start.1 = ((bf16[128,10,4096]{2,1,0:T(8,128)(2,1)}), bf16[128,10,4096]{2,1,0:T(8,128)(2,1)}, u32[]{:S(2)}, u32[]{:S(2)}) async-start(bf16[128,10,4096]{2,1,0:T(8,128)(2,1)} %reshape.137), calls=%async_computation.1 | async-start | bytes 33554432 | tf_op jit(solution)/shard_map/all_to_all | solution.py:29
  76.4 0.2 convert_reduce_fusion
  76.6 0.1 reshape.141
  76.7 221.4 %all-to-all-done.1 = bf16[128,10,4096]{2,1,0:T(8,128)(2,1)} async-done(((bf16[128,10,4096]{2,1,0:T(8,128)(2,1)}), bf16[128,10,4096]{2,1,0:T(8,128)(2,1)}, u32[]{:S(2)}, u32[]{:S(2)}) %all-to-all-start.1) | async-done | bytes 10485792 | tf_op jit(solution)/shard_map/all_to_all | solution.py:29
  298.1 16.5 %reshape.138 = bf16[1280,4096]{1,0:T(8,128)(2,1)} reshape(bf16[128,10,4096]{2,1,0:T(8,128)(2,1)} %all-to-all-done.1) | data formatting | bytes 20971520 | tf_op jit(solution)/shard_map/reshape | solution.py:44
  314.6 24.3 %fusion.2 = (f32[1280]{0:T(1024)S(1)}, bf16[1,1280,1536]{2,1,0:T(8,128)(2,1)}) fusion(bf16[1,1280,1536]{2,1,0:T(8,128)(2,1)} %param.8, f32[1280]{0:T(1024)S(1)} %reshape.141, bf16[1280,4096]{1,0:T(8,128)(2,1)} %reshape.138, bf16[1,1536,4096]{2,1,0:T(8,128)(2,1)} %param.9), kind=kOutput, calls=%fused_computation.7 | convolution fusion | flops 16115956736 | bytes 30943232 | tf_op jit(solution)/shard_map/dot_general | solution.py:46
  338.9 0.8 all_to_all.18
  339.6 12.9 %all-to-all-start.2 = ((f32[128,1,10]{2,1,0:T(1,128)}), f32[128,1,10]{2,1,0:T(1,128)S(1)}, u32[]{:S(2)}, u32[]{:S(2)}) async-start(f32[128,1,10]{2,1,0:T(1,128)} %bitcast.9), calls=%async_computation.2 | async-start | bytes 131072 | tf_op jit(solution)/shard_map/all_to_all | solution.py:51
  352.5 9.9 %all-to-all-done.2 = f32[128,1,10]{2,1,0:T(1,128)S(1)} async-done(((f32[128,1,10]{2,1,0:T(1,128)}), f32[128,1,10]{2,1,0:T(1,128)S(1)}, u32[]{:S(2)}, u32[]{:S(2)}) %all-to-all-start.2) | async-done | bytes 5152 | tf_op jit(solution)/shard_map/all_to_all | solution.py:51
  362.4 0.5 broadcast.142
  362.9 0.8 reduce.7
  363.8 0.1 reshape.139
  363.9 6.2 %gather_fusion.1 = f32[1024]{0:T(1024)S(1)} fusion(f32[1280]{0:T(1024)S(1)} %reshape.139, s32[1024]{0:T(1024)S(1)} %broadcast_clamp_fusion), kind=kCustom, calls=%fused_computation.1 | custom fusion | bytes 12288 | tf_op jit(solution)/shard_map/gather | solution.py:58
  370.1 0.7 copy.22
  (15 shorter events, 0.2 us)
Async XLA Ops:
  0.6 23.7 %copy-start = (bf16[128,4096]{1,0:T(8,128)(2,1)S(1)}, bf16[128,4096]{1,0:T(8,128)(2,1)}, u32[]{:S(2)}) copy-start(bf16[128,4096]{1,0:T(8,128)(2,1)} %param.5) | copy-start | bytes 3145732
  12.8 53.4 %all-to-all-start = ((bf16[128,1,10]{2,1,0:T(2,128)(2,1)}), bf16[128,1,10]{2,1,0:T(2,128)(2,1)S(1)}, u32[]{:S(2)}, u32[]{:S(2)}) async-start(bf16[128,1,10]{2,1,0:T(2,128)(2,1)} %all_to_all.20), calls=%async_computation | async-start | bytes 131072 | tf_op jit(solution)/shard_map/all_to_all | solution.py:36
  66.2 231.9 %all-to-all-start.1 = ((bf16[128,10,4096]{2,1,0:T(8,128)(2,1)}), bf16[128,10,4096]{2,1,0:T(8,128)(2,1)}, u32[]{:S(2)}, u32[]{:S(2)}) async-start(bf16[128,10,4096]{2,1,0:T(8,128)(2,1)} %reshape.137), calls=%async_computation.1 | async-start | bytes 33554432 | tf_op jit(solution)/shard_map/all_to_all | solution.py:29
  314.6 56.2 %copy-start.1 = (bf16[128,4096]{1,0:T(8,128)(2,1)S(1)}, bf16[128,4096]{1,0:T(8,128)(2,1)}, u32[]{:S(2)}) copy-start(bf16[128,4096]{1,0:T(8,128)(2,1)} %param.5) | copy-start | bytes 3145732
  339.6 22.8 %all-to-all-start.2 = ((f32[128,1,10]{2,1,0:T(1,128)}), f32[128,1,10]{2,1,0:T(1,128)S(1)}, u32[]{:S(2)}, u32[]{:S(2)}) async-start(f32[128,1,10]{2,1,0:T(1,128)} %bitcast.9), calls=%async_computation.2 | async-start | bytes 131072 | tf_op jit(solution)/shard_map/all_to_all | solution.py:51
where the time goes:
time: 372 us; the launch traced here: 371 us
  waiting for transfers between devices  231 us (62%)
  local copies, waits for them, and re-layouts  77.5 us (21%)
  starting transfers between devices  34.6 us (9%)
  matrix products  24.3 us (7%)
    all_to_all x1, waiting for transfers between devices, per_device(): lax.all_to_all(send_grad.reshape(experts_count, capacity, width), ('ctx',...  221 us
    dot_general x1, matrix products, per_device(): lax.dot_general(slot_grad, down_weight[0], (((1,), (1,)), ((), ())), pref...  24.3 us
    scatter x1, local copies, waits for them, and re-layouts, per_device(): jnp.zeros((slot_rows, width), jnp.bfloat16).at[slot_index]  18.8 us
    reshape x1, local copies, waits for them, and re-layouts, per_device(): slot_grad = recv_grad.reshape(slot_rows, width)  16.5 us
    reshape x1, local copies, waits for them, and re-layouts, per_device(): send_grad.reshape(experts_count, capacity, width)  15.2 us
    all_to_all x1, starting transfers between devices, per_device(): lax.all_to_all(slot_back.reshape(experts_count, capacity), ('ctx', 'tp'),...  12.9 us
    all_to_all x1, starting transfers between devices, per_device(): lax.all_to_all(send_weight.reshape(experts_count, capacity), ('ctx', 'tp'...  11.5 us
    all_to_all x1, starting transfers between devices, per_device(): lax.all_to_all(send_grad.reshape(experts_count, capacity, width), ('ctx',...  10.2 us
  transfers between devices with their start and end apart: 3, of which 2 were waited for; matrix products, arithmetic and copies ran while one was open for 11% of the time, Pallas kernels for 0%

commit v1 on v0

v1 whole, which is shorter than its diff:
```python
import jax
import jax.numpy as jnp
from jax import lax
from jax.experimental import pallas as pl
from jax.experimental.pallas import tpu as pltpu
from jax.sharding import PartitionSpec as P

MESH = pl.DeviceIdType.MESH
F32 = jnp.float32
BF16 = jnp.bfloat16
CAP = 10
PARTS = (0, 1, 2)


def place(z, y, x, c):
    return ((z // 2) * 4 + y, (z % 2) * 8 + x * 2 + c)


def number(z, y, x, c):
    return (z // 2) * 64 + y * 16 + (z % 2) * 8 + x * 2 + c


def iota(shape, dim):
    return lax.broadcasted_iota(jnp.int32, shape, dim)


def div(a, b):
    return lax.div(a, jnp.int32(b))


def rem(a, b):
    return lax.rem(a, jnp.int32(b))


def dot(a, b):
    return lax.dot_general(a, b, (((1,), (0,)), ((), ())), preferred_element_type=F32)


def dot_t(a, b):
    return lax.dot_general(a, b, (((1,), (1,)), ((), ())), preferred_element_type=F32)


def kernel(
    halves, starts, ff,
    table_ref, grad_ref, saved_ref, weight_ref,
    out_ref, comb_ref,
    ag0, ag1, ag2, ids, pos, snd0, snd1, snd2, rcv0, rcv1, rcv2, y0, y1, y2,
    perm, wv, raw, hs, cws, cwr, sbs, sbr,
    s_ag, r_ag, s_id, r_id, s_mv, r_mv, s_cw, r_cw, s_sb, r_sb, l_w, l_hs, l_out, l_own,
):
    ag, snd, rcv, yb = (ag0, ag1, ag2), (snd0, snd1, snd2), (rcv0, rcv1, rcv2), (y0, y1, y2)
    ctx, tp = lax.axis_index("ctx"), lax.axis_index("tp")
    z, y, x, c = (ctx // 4) * 2 + tp // 8, ctx % 4, (tp // 2) % 4, tp % 2
    me = ctx * 16 + tp
    at = (z, y, x)

    def mate(p, d):
        return place(*(((v + d) % 4 if q == p else v) for q, v in enumerate((z, y, x))), c)

    def other(i):
        return place((z + i // 32) % 4, (y + (i // 8) % 4) % 4, (x + (i // 2) % 4) % 4, (c + i % 2) % 2)

    barrier = pltpu.get_barrier_semaphore()

    def greet(i, _):
        pl.semaphore_signal(barrier, inc=1, device_id=other(i), device_id_type=MESH)
        return 0

    lax.fori_loop(1, 128, greet, 0)

    own = []
    for p in PARTS:
        cols = pl.ds(starts[p], 2 * halves[p])
        own.append(pltpu.make_async_copy(grad_ref.at[:, cols], ag[p].at[at[p]], l_own.at[p]))
        own[-1].start()
    load_w = pltpu.make_async_copy(weight_ref.at[0], wv, l_w)
    load_w.start()
    load_hs = pltpu.make_async_copy(saved_ref.at[0], hs, l_hs)
    load_hs.start()
    for p in PARTS:
        ids[p, at[p]] = table_ref[:8, :]

    for q in range(2):
        row = iota((640, 1), 0)
        chunk, b, g, j = div(row, 320), rem(div(row, 80), 4), rem(div(row, 10), 8), rem(row, 10)
        if q == 0:
            source = g * 80 + chunk * 40 + b * 10 + j
        else:
            source = (b * 2 + rem(g, 2)) * 80 + chunk * 40 + div(g, 2) * 10 + j
        perm[q] = jnp.where(iota((640, 640), 1) == source, 1.0, 0.0).astype(BF16)

    before = jnp.where(iota((128, 128), 0) < iota((128, 128), 1), 1.0, 0.0).astype(BF16)
    expert = iota((128, 128), 0).astype(F32)

    def positions(table):
        named = jnp.zeros((128, 128), F32)
        for k in range(8):
            named = named + jnp.where(expert == table[k : k + 1, :], 1.0, 0.0)
        earlier = dot(named.astype(BF16), before)
        return jnp.where(named > 0.0, earlier, -1.0)

    table = table_ref[...]
    mine = positions(table[:8, :])
    scale = jnp.zeros((128, 128), F32)
    for k in range(8):
        scale = scale + jnp.where(expert == table[k : k + 1, :], table[8 + k : 9 + k, :], 0.0)
    lane = iota((128, 128), 1)
    rows = jnp.zeros((128, 128), F32)
    for j in range(CAP):
        column = jnp.sum(jnp.where(mine == float(j), scale, 0.0), axis=1, keepdims=True)
        rows = rows + jnp.where(lane == j, column, 0.0)
    cws[...] = rows.reshape(128, 1, 128)

    pl.semaphore_wait(barrier, 127)

    def gather(p, d):
        cols = pl.ds(starts[p], 2 * halves[p])
        return pltpu.make_async_remote_copy(
            grad_ref.at[:, cols], ag[p].at[at[p]], s_ag.at[p, d], r_ag.at[p, at[p]],
            device_id=mate(p, d), device_id_type=MESH,
        )

    def gather_ids(p, d):
        return pltpu.make_async_remote_copy(
            table_ref.at[pl.ds(0, 8)], ids.at[p, at[p]], s_id.at[p, d], r_id.at[p, at[p]],
            device_id=mate(p, d), device_id_type=MESH,
        )

    for d in (1, 3, 2):
        for p in PARTS:
            gather_ids(p, d).start()
    for d in (1, 3, 2):
        for p in PARTS:
            gather(p, d).start()

    def send_cw(i):
        d = other(i)
        return pltpu.make_async_remote_copy(
            cws.at[d[0] * 16 + d[1]], cwr.at[me], s_cw, r_cw, device_id=d, device_id_type=MESH
        )

    lax.fori_loop(1, 128, lambda i, _: (send_cw(i).start(), 0)[1], 0)
    cwr[me] = cws[me]

    for p in PARTS:
        for d in (1, 2, 3):
            b = (at[p] + d) % 4
            pltpu.make_async_remote_copy(
                table_ref.at[pl.ds(0, 8)], ids.at[p, b], s_id.at[p, d], r_id.at[p, b],
                device_id=mate(p, d), device_id_type=MESH,
            ).wait_recv()
    for p in PARTS:
        for b in range(4):
            pos[p, :, b * 128 : (b + 1) * 128] = positions(ids[p, b]).astype(BF16)

    raw[...] = jnp.zeros_like(raw)

    for p in PARTS:
        own[p].wait()
    for d in (1, 3, 2):
        for p in PARTS:
            b = (at[p] + d) % 4
            cols = pl.ds(starts[p], 2 * halves[p])
            pltpu.make_async_remote_copy(
                grad_ref.at[:, cols], ag[p].at[b], s_ag.at[p, d], r_ag.at[p, b],
                device_id=mate(p, d), device_id_type=MESH,
            ).wait_recv()

    slot = (y * 8 + x * 2 + c, z * 8 + x * 2 + c, y * 8 + z * 2 + c)

    def target(p, k, g):
        d = (k + 1) % 4
        if p == 0:
            return (z, (y + d) % 4, g // 2, g % 2)
        if p == 1:
            return ((z + d) % 4, y, g // 2, g % 2)
        return (g // 2, (y + d) % 4, x, g % 2)

    def move(p, k, g):
        return pltpu.make_async_remote_copy(
            snd[p].at[k * 8 + g], rcv[p].at[slot[p]], s_mv.at[p, k * 8 + g], r_mv.at[p, slot[p]],
            device_id=place(*target(p, k, g)), device_id_type=MESH,
        )

    def keep(p, g):
        return pltpu.make_async_copy(snd[p].at[24 + g], rcv[p].at[slot[p]], r_mv.at[p, slot[p]])

    def pick(k, p):
        row = iota((320, 1), 0)
        e, b, j = div(row, 40), rem(div(row, 10), 4), rem(row, 10)
        if p == 2:
            who = number(div(e, 2), target(p, k, 0)[1], x, rem(e, 2))
        else:
            first = target(p, k, 0)
            who = number(first[0], first[1], 0, 0) + e
        chosen = jnp.where(iota((320, 128), 1) == who, 1.0, 0.0).astype(BF16)
        value = dot(chosen, pos[p])
        hit = (value == j.astype(F32)) & (div(iota((1, 512), 1), 128) == b)
        onehot = jnp.where(hit, 1.0, 0.0).astype(BF16)
        h = halves[p]
        parts = [dot(onehot, ag[p][:, :, i * h : (i + 1) * h].reshape(512, h)) for i in range(2)]
        for g in range(8):
            both = [part[g * 40 : g * 40 + 40] for part in parts]
            snd[p][k * 8 + g] = jnp.concatenate(both, axis=0).astype(BF16)

    def send_stage(k, _):
        for p in PARTS:
            pick(k, p)

        def send(i, _):
            for p in PARTS:
                a = (z if p == 2 else x) + i + 1 + k
                g = (a % 4) * 2 + (c + i // 4) % 2

                if p == 2:
                    itself = (k == 3) & (g == z * 2 + c)
                else:
                    itself = (k == 3) & (g == x * 2 + c)

                @pl.when(itself)
                def _():
                    keep(p, g).start()

                @pl.when(jnp.logical_not(itself))
                def _():
                    move(p, k, g).start()
            return 0

        return lax.fori_loop(0, 8, send, 0)

    lax.fori_loop(0, 4, send_stage, 0)

    load_w.wait()
    load_hs.wait()
    pltpu.make_async_remote_copy(
        cws.at[pl.ds(0, 127)], cwr.at[pl.ds(0, 127)], s_cw, r_cw, device_id=other(1), device_id_type=MESH
    ).wait_recv()

    def arrive(p, k):
        d = (k + 1) % 4
        block = ((y + 4 - d) % 4, (z + 4 - d) % 4, (y + 4 - d) % 4)[p]

        def wait(g, _):
            i = block * 8 + g
            pltpu.make_async_copy(snd[p].at[0], rcv[p].at[i], r_mv.at[p, i]).wait()
            return 0

        lax.fori_loop(0, 8, wait, 0)
        h = halves[p]
        got = rcv[p][pl.ds(block * 8, 8)].reshape(640, h)
        yb[p][...] = dot(perm[1 if p == 2 else 0], got).astype(BF16)
        return block

    step = 512

    def back(unit_y, unit_z):
        first = number(unit_z, unit_y, 0, 0)
        here = pl.ds(pl.multiple_of((unit_y * 4 + unit_z) * 80, 80), 80)
        there = pl.ds(pl.multiple_of(first * CAP, 80), 80)
        row = iota((80, 1), 0)
        j = rem(row, 10)
        lanes = iota((80, 128), 1)
        spread = jnp.where(iota((80, 8), 1) == div(row, 10), 1.0, 0.0)
        weights = dot(spread.astype(BF16), cwr[pl.ds(first, 8)].reshape(8, 128).astype(BF16))
        weight = jnp.sum(jnp.where(lanes == j, weights, 0.0), axis=1, keepdims=True)
        total = raw[here, :]
        summed = jnp.sum(hs[there, :].astype(F32) * total, axis=1, keepdims=True)
        hs[there, :] = (weight * total).astype(BF16)
        pltpu.make_async_copy(hs.at[there], out_ref.at[0, there], l_out.at[unit_y * 4 + unit_z]).start()
        cells = jnp.where(lanes == j, summed, 0.0)
        for g in range(8):
            line = jnp.sum(cells[g * 10 : g * 10 + 10, :], axis=0, keepdims=True)
            sbs[first + g] = line

            @pl.when(first + g == me)
            def _():
                sbr[me] = line

            @pl.when(first + g != me)
            def _():
                pltpu.make_async_remote_copy(
                    sbs.at[first + g], sbr.at[me], s_sb, r_sb,
                    device_id=place(unit_z, unit_y, g // 2, g % 2), device_id_type=MESH,
                ).start()

    def receive_stage(k, _):
        y_block = arrive(0, k)
        arrive(2, k)
        here = pl.ds(pl.multiple_of(y_block * 320, 320), 320)

        def multiply(n, _):
            out = pl.ds(pl.multiple_of(n * step, step), step)
            acc = jnp.zeros((320, step), F32)
            for p in (0, 2):
                h = halves[p]
                for i in range(2):
                    w = wv[out, starts[p] + i * h : starts[p] + (i + 1) * h]
                    acc = acc + dot_t(yb[p][i * 320 : (i + 1) * 320, :], w)
            raw[here, out] += acc
            return 0

        lax.fori_loop(0, ff // step, multiply, 0)
        z_block = arrive(1, k)

        def multiply_y(n, _):
            out = pl.ds(pl.multiple_of(n * step, step), step)
            acc = jnp.zeros((320, step), F32)
            h = halves[1]
            for i in range(2):
                w = wv[out, starts[1] + i * h : starts[1] + (i + 1) * h]
                acc = acc + dot_t(yb[1][i * 320 : (i + 1) * 320, :], w)
            for b in range(4):
                rows_b = pl.ds(pl.multiple_of(b * 320 + z_block * 80, 80), 80)
                raw[rows_b, out] += acc[b * 80 : (b + 1) * 80]
            return 0

        lax.fori_loop(0, ff // step, multiply_y, 0)

        def finish(i, _):
            back(y_block, (z + 4 - (i + 1) % 4) % 4)
            return 0

        lax.fori_loop(0, k + 1, finish, 0)

        def finish_z(i, _):
            back((y + 4 - (i + 1) % 4) % 4, z_block)
            return 0

        lax.fori_loop(0, k, finish_z, 0)
        return 0

    lax.fori_loop(0, 4, receive_stage, 0)

    pltpu.make_async_remote_copy(
        sbs.at[pl.ds(0, 127)], sbr.at[pl.ds(0, 127)], s_sb, r_sb, device_id=other(1), device_id_type=MESH
    ).wait_recv()
    returned = sbr[...].reshape(128, 128)
    found = jnp.zeros((128, 128), F32)
    for j in range(CAP):
        found = found + jnp.where(mine == float(j), returned[:, j : j + 1], 0.0)
    for k in range(8):
        chosen = jnp.where(expert == table[k : k + 1, :], found, 0.0)
        comb_ref[k : k + 1, :] = jnp.sum(chosen, axis=0, keepdims=True)

    for d in (1, 3, 2):
        for p in PARTS:
            gather(p, d).wait_send()
            gather_ids(p, d).wait_send()
    pltpu.make_async_remote_copy(
        cws.at[pl.ds(0, 127)], cwr.at[pl.ds(0, 127)], s_cw, r_cw, device_id=other(1), device_id_type=MESH
    ).wait_send()
    pltpu.make_async_remote_copy(
        sbs.at[pl.ds(0, 127)], sbr.at[pl.ds(0, 127)], s_sb, r_sb, device_id=other(1), device_id_type=MESH
    ).wait_send()

    def sent(i, _):
        for p in PARTS:
            g = i % 8
            itself = (i // 8 == 3) & (g == (z if p == 2 else x) * 2 + c)

            @pl.when(jnp.logical_not(itself))
            def _():
                move(p, i // 8, g).wait_send()
        return 0

    lax.fori_loop(0, 32, sent, 0)

    def stored(u, _):
        pltpu.make_async_copy(hs.at[pl.ds(0, 80)], out_ref.at[0, pl.ds(0, 80)], l_out.at[u]).wait()
        return 0

    lax.fori_loop(0, 16, stored, 0)


def per_device(out_grad, combine_weights, expert_ids, hidden_saved, down_weight):
    slots, ff = hidden_saved.shape[1:]
    units = out_grad.shape[1] // 256
    counts = [(units + i) // 3 for i in range(3)]
    halves = tuple(128 * n for n in counts)
    starts = (0, 2 * halves[0], 2 * (halves[0] + halves[1]))
    table = jnp.concatenate([expert_ids.T.astype(F32), combine_weights.T.astype(F32)], axis=0)
    anywhere = pl.BlockSpec(memory_space=pl.ANY)
    vmem = pl.BlockSpec(memory_space=pltpu.VMEM)
    dma = pltpu.SemaphoreType.DMA

    def body(*refs):
        kernel(halves, starts, ff, *refs)

    hidden_grad, combine = pl.pallas_call(
        body,
        out_shape=(
            jax.ShapeDtypeStruct(hidden_saved.shape, BF16),
            jax.ShapeDtypeStruct((8, 128), F32),
        ),
        in_specs=[vmem, anywhere, anywhere, anywhere],
        out_specs=(anywhere, vmem),
        scratch_shapes=[pltpu.VMEM((4, 128, 2 * h), BF16) for h in halves]
        + [pltpu.VMEM((3, 4, 8, 128), F32), pltpu.VMEM((3, 128, 512), BF16)]
        + [pltpu.VMEM((32, 80, h), BF16) for h in halves] * 2
        + [pltpu.VMEM((640, h), BF16) for h in halves]
        + [
            pltpu.VMEM((2, 640, 640), BF16),
            pltpu.VMEM((ff, out_grad.shape[1]), BF16),
            pltpu.VMEM((slots, ff), F32),
            pltpu.VMEM((slots, ff), BF16),
        ]
        + [pltpu.VMEM((128, 1, 128), F32)] * 4
        + [dma((3, 4))] * 4
        + [dma((3, 32))] * 2
        + [dma] * 6
        + [dma((16,)), dma((3,))],
        compiler_params=pltpu.CompilerParams(
            collective_id=0, has_side_effects=True, vmem_limit_bytes=62 << 20
        ),
    )(table, out_grad, hidden_saved, down_weight)
    return hidden_grad, combine.T


def solution(mesh):
    both = ("ctx", "tp")
    in_specs = (P(both, None), P(both, None), P(both, None), P(both, None, None), P(both, None, None))
    out_specs = (P(both, None, None), P(both, None))
    return jax.shard_map(
        per_device, mesh=mesh, in_specs=in_specs, out_specs=out_specs, check_vma=False
    )
```

time: 372 us -> 180 us (0.48)
  waiting for transfers between devices: 231 us -> 0 us
  Pallas kernels: 0 us -> 173 us
  local copies, waits for them, and re-layouts: 77.5 us -> 4.89 us
  starting transfers between devices: 34.6 us -> 0 us
  matrix products: 24.3 us -> 0 us
    all_to_all x3 -> x0, waiting for transfers between devices: 231 us -> none  [the longest x1 221 us: per_device(): lax.all_to_all(send_grad.reshape(experts_count, capacity, width), ('ctx',...]
    pallas_call x0 -> x1, Pallas kernels: none -> 173 us  [per_device(): pl.pallas_call(body, out_shape=(jax.ShapeDtypeStruct(hidden_saved.shape,...]
    all_to_all x3 -> x0, starting transfers between devices: 34.6 us -> none  [the longest x1 12.9 us: per_device(): lax.all_to_all(slot_back.reshape(experts_count, capacity), ('ctx', 'tp'),...]
    reshape x5 -> x0, local copies, waits for them, and re-layouts: 32 us -> none  [the longest x1 16.5 us: per_device(): slot_grad = recv_grad.reshape(slot_rows, width)]
    scatter x2 -> x0, local copies, waits for them, and re-layouts: 26.4 us -> none  [the longest x1 18.8 us: per_device(): jnp.zeros((slot_rows, width), jnp.bfloat16).at[slot_index]]
    dot_general x1 -> x0, matrix products: 24.3 us -> none  [per_device(): lax.dot_general(slot_grad, down_weight[0], (((1,), (1,)), ((), ())), pref...]
    gather x2 -> x0, local copies, waits for them, and re-layouts: 13.9 us -> none  [the longest x1 7.79 us: per_device(): out_grad[token_index]]
  transfers between devices with their start and end apart: 3 -> 0, of which waited for: 2 -> 0; matrix products, arithmetic and copies ran while one was open for 11% -> 0% of each run, Pallas kernels for 0% -> 0%
where the time goes in v1:
time: 180 us
  Pallas kernels  173 us (96%)
  local copies, waits for them, and re-layouts  4.89 us (3%)
  other arithmetic  1.98 us (1%)
    pallas_call x1, Pallas kernels, per_device(): pl.pallas_call(body, out_shape=(jax.ShapeDtypeStruct(hidden_saved.shape,...  173 us
    unnamed x4, local copies, waits for them, and re-layouts  4.89 us

profile of v1, /device:TPU:1, one launch (start us, length us, event | category | flops | bytes accessed | tf_op | source)
XLA Modules:
  0.0 180.2 jit_solution(1494326864492738935)
XLA Ops:
  0.6 0.7 convert_bitcast_fusion
  1.3 0.7 convert_bitcast_fusion.1
  2.0 0.6 pad_maximum_fusion.refs_0_
  2.6 172.7 %shard_map.68 = (bf16[1,1280,1536]{2,1,0:T(8,128)(2,1)}, f32[8,128]{1,0:T(8,128)}) custom-call(f32[16,128]{1,0:T(8,128)} %pad_maximum_fusion.refs_0_, bf16[128,4096]{1,0:T(8,128)(2,1)} %refs_1_.1, bf16[1,1280,1536]{2,1,0:T(8,128)(2,1)} %refs_2_.1, bf16[1,1536,4096]{2,1,0:T(8,128)(2,1)} %refs_3_.1), custom_call_target="tpu_custom_call" | custom-call | tf_op jit(solution)/shard_map/pallas_call | solution.py:389
  175.3 0.0 copy-start
  175.3 4.3 %copy.9 = bf16[1,1280,1536]{2,1,0:T(8,128)(2,1)} copy(bf16[1,1280,1536]{2,1,0:T(8,128)(2,1)} %get-tuple-element.8) | data formatting | bytes 7864320
  179.6 0.0 copy-done
  179.6 0.6 copy.10
Async XLA Ops:
  175.3 4.3 %copy-start = (f32[8,128]{1,0:T(8,128)S(1)}, f32[8,128]{1,0:T(8,128)}, u32[]{:S(2)}) copy-start(f32[8,128]{1,0:T(8,128)} %get-tuple-element.5) | copy-start | bytes 12292

commit v2 on v1

v2 whole, which is shorter than its diff:
```python
import jax
import jax.numpy as jnp
from jax import lax
from jax.experimental import pallas as pl
from jax.experimental.pallas import tpu as pltpu
from jax.sharding import PartitionSpec as P

MESH = pl.DeviceIdType.MESH
F32 = jnp.float32
BF16 = jnp.bfloat16
CAP = 10
AXES = (0, 1, 2)
SETS = (0, 1, 2)
SHARES = ((2, 2, 2), (2, 2, 2), (1, 1, 2))


def place(z, y, x, c):
    return ((z // 2) * 4 + y, (z % 2) * 8 + x * 2 + c)


def number(z, y, x, c):
    return (z // 2) * 64 + y * 16 + (z % 2) * 8 + x * 2 + c


def iota(shape, dim):
    return lax.broadcasted_iota(jnp.int32, shape, dim)


def div(a, b):
    return lax.div(a, jnp.int32(b))


def rem(a, b):
    return lax.rem(a, jnp.int32(b))


def dot(a, b):
    return lax.dot_general(a, b, (((1,), (0,)), ((), ())), preferred_element_type=F32)


def dot_t(a, b):
    return lax.dot_general(a, b, (((1,), (1,)), ((), ())), preferred_element_type=F32)


def kernel(halves, starts, ff, ids_ref, scale_ref, grad_ref, saved_ref, weight_ref, out_ref, comb_ref, *scratch):
    scratch = list(scratch)

    def take(n):
        got = scratch[:n]
        del scratch[:n]
        return got

    ag, snd, rcv = ([take(3) for _ in SETS] for _ in range(3))
    yb = take(3)
    ids, pos, zpos, perm, wv, raw, hs, cws, cwr, sbs, sbr = take(11)
    s_ag, r_ag, s_id, r_id, s_mv, r_mv, s_cw, r_cw, s_sb, r_sb, l_w, l_hs, l_out, l_own = take(14)

    ctx, tp = lax.axis_index("ctx"), lax.axis_index("tp")
    z, y, x, c = (ctx // 4) * 2 + tp // 8, ctx % 4, (tp // 2) % 4, tp % 2
    me = ctx * 16 + tp
    at = (z, y, x)
    slot = (y * 8 + x * 2 + c, z * 8 + x * 2 + c, y * 8 + z * 2 + c)

    def mate(p, d, core):
        return place(*(((v + d) % 4 if q == p else v) for q, v in enumerate(at)), core)

    barrier = pltpu.get_barrier_semaphore()
    for d in (1, 3, 2):
        for p in AXES:
            for core in (c, 1 - c):
                pl.semaphore_signal(barrier, inc=1, device_id=mate(p, d, core), device_id_type=MESH)
    pl.semaphore_signal(barrier, inc=1, device_id=place(z, y, x, 1 - c), device_id_type=MESH)

    own = []
    for s in SETS:
        for p in AXES:
            cols = pl.ds(starts[s][p], 2 * halves[s][p])
            own.append(pltpu.make_async_copy(grad_ref.at[:, cols], ag[s][p].at[at[p]], l_own.at[s * 3 + p]))
            own[-1].start()
    load_w = pltpu.make_async_copy(weight_ref.at[0], wv, l_w)
    load_hs = pltpu.make_async_copy(saved_ref.at[0], hs, l_hs)

    ids_t = ids_ref[...].astype(F32)
    scale_t = scale_ref[...].astype(F32)
    for p in AXES:
        ids[p * 4 + at[p], :8, :] = ids_t
        ids[p * 4 + at[p], 8:, :] = scale_t
    for copy in own:
        copy.wait()
    pl.semaphore_wait(barrier, 19)

    def gather(s, p, d):
        here = ag[s][p].at[at[p]]
        return pltpu.make_async_remote_copy(
            here, here, s_ag.at[s * 3 + p, d], r_ag.at[s * 3 + p, d], device_id=mate(p, d, c), device_id_type=MESH
        )

    def forward(s, p, d):
        half = ag[s][p].at[(at[p] + 4 - d) % 4, pl.ds(64 * (d // 2), 64)]
        return pltpu.make_async_remote_copy(
            half, half, s_ag.at[s * 3 + p, d - 1], r_ag.at[s * 3 + p, d - 1],
            device_id=mate(p, d, c), device_id_type=MESH,
        )

    def gather_ids(p, d):
        here = ids.at[p * 4 + at[p]]
        return pltpu.make_async_remote_copy(
            here, here, s_id, r_id, device_id=mate(p, d, c), device_id_type=MESH
        )

    for d in (1, 3, 2):
        for p in AXES:
            gather_ids(p, d).start()
    for s in SETS:
        for d in (1, 3):
            for p in AXES:
                gather(s, p, d).start()
    load_w.start()
    load_hs.start()

    for q in range(2):
        row = iota((640, 1), 0)
        chunk, b, g, j = div(row, 320), rem(div(row, 80), 4), rem(div(row, 10), 8), rem(row, 10)
        if q == 0:
            source = g * 80 + chunk * 40 + b * 10 + j
        else:
            source = (b * 2 + rem(g, 2)) * 80 + chunk * 40 + div(g, 2) * 10 + j
        perm[q] = jnp.where(iota((640, 640), 1) == source, 1.0, 0.0).astype(BF16)
    raw[...] = jnp.zeros_like(raw)

    before = jnp.where(iota((128, 128), 0) < iota((128, 128), 1), 1.0, 0.0).astype(BF16)
    expert = iota((128, 128), 0).astype(F32)

    def positions(table):
        named = jnp.zeros((128, 128), F32)
        for k in range(8):
            named = named + jnp.where(expert == table[k : k + 1, :], 1.0, 0.0)
        earlier = dot(named.astype(BF16), before)
        return jnp.where(named > 0.0, earlier, -1.0)

    nine = ids.at[pl.ds(0, 9)]
    pltpu.make_async_copy(nine, nine, r_id).wait()
    for p in AXES:
        for b in range(4):
            found = positions(ids[p * 4 + b])
            pos[p, :, b * 128 : (b + 1) * 128] = found.astype(BF16)
            if p == 0:
                zpos[b] = found

    lane8 = iota((8, 128), 1)

    def weigh(unit_y, _):
        first = pl.multiple_of(number(z, unit_y, 0, 0), 8)
        named = (iota((8, 128), 0) + first).astype(F32)
        rows = jnp.zeros((8, 128), F32)
        for b in range(4):
            scale = jnp.zeros((8, 128), F32)
            for k in range(8):
                scale = scale + jnp.where(named == ids[b, k : k + 1, :], ids[b, 8 + k : 9 + k, :], 0.0)
            which = zpos[b, pl.ds(first, 8), :]
            for j in range(CAP):
                column = jnp.sum(jnp.where(which == float(j), scale, 0.0), axis=1, keepdims=True)
                rows = rows + jnp.where(lane8 == b * CAP + j, column, 0.0)
        for g in range(8):
            cws[unit_y * 8 + g] = rows[g : g + 1]
        return 0

    lax.fori_loop(0, 4, weigh, 0)

    def relay(s):
        for d in (1, 3):
            for p in AXES:
                gather(s, p, d).wait_recv()
                forward(s, p, d).start()

    def arrived(s):
        for d in (1, 3):
            for p in AXES:
                forward(s, p, d).wait_recv()

    def target(p, k, g):
        d = (k + 1) % 4
        if p == 0:
            return (z, (y + d) % 4, g // 2, g % 2)
        if p == 1:
            return ((z + d) % 4, y, g // 2, g % 2)
        return (g // 2, (y + d) % 4, x, g % 2)

    def move(s, p, k, g):
        return pltpu.make_async_remote_copy(
            snd[s][p].at[k * 8 + g], rcv[s][p].at[slot[p]], s_mv.at[s, p * 4 + k],
            r_mv.at[s, p * 4 + slot[p] // 8],
            device_id=place(*target(p, k, g)), device_id_type=MESH,
        )

    def keep(s, p, g):
        return pltpu.make_async_copy(
            snd[s][p].at[24 + g], rcv[s][p].at[slot[p]], r_mv.at[s, p * 4 + slot[p] // 8]
        )

    def pick(s, k, p):
        row = iota((320, 1), 0)
        e, b, j = div(row, 40), rem(div(row, 10), 4), rem(row, 10)
        first = target(p, k, 0)
        if p == 2:
            who = number(div(e, 2), first[1], x, rem(e, 2))
        else:
            who = number(first[0], first[1], 0, 0) + e
        chosen = jnp.where(iota((320, 128), 1) == who, 1.0, 0.0).astype(BF16)
        value = dot(chosen, pos[p])
        hit = (value == j.astype(F32)) & (div(iota((1, 512), 1), 128) == b)
        onehot = jnp.where(hit, 1.0, 0.0).astype(BF16)
        h = halves[s][p]
        parts = [dot(onehot, ag[s][p][:, :, i * h : (i + 1) * h].reshape(512, h)) for i in range(2)]
        for g in range(8):
            both = [part[g * 40 : g * 40 + 40] for part in parts]
            snd[s][p][k * 8 + g] = jnp.concatenate(both, axis=0).astype(BF16)

    def send_stage(s, k):
        for p in AXES:
            pick(s, k, p)

        def send(i, _):
            for p in AXES:
                own_g = (z if p == 2 else x) * 2 + c
                g = (((z if p == 2 else x) + i + 1 + k) % 4) * 2 + (c + i // 4) % 2
                itself = (k == 3) & (g == own_g)

                @pl.when(itself)
                def _():
                    keep(s, p, g).start()

                @pl.when(jnp.logical_not(itself))
                def _():
                    move(s, p, k, g).start()
            return 0

        lax.fori_loop(0, 8, send, 0)

    def sent(s, k):
        for p in AXES:
            eight, seven = snd[s][p].at[pl.ds(0, 8)], snd[s][p].at[pl.ds(0, 7)]

            @pl.when(k < 3)
            def _():
                pltpu.make_async_copy(eight, eight, s_mv.at[s, p * 4 + k]).wait()

            @pl.when(k == 3)
            def _():
                pltpu.make_async_copy(seven, seven, s_mv.at[s, p * 4 + k]).wait()

    def arrive(s, p, k):
        d = (k + 1) % 4
        block = ((y + 4 - d) % 4, (z + 4 - d) % 4, (y + 4 - d) % 4)[p]
        rows = rcv[s][p].at[pl.ds(block * 8, 8)]
        pltpu.make_async_copy(rows, rows, r_mv.at[s, p * 4 + block]).wait()
        h = halves[s][p]
        got = rcv[s][p][pl.ds(block * 8, 8)].reshape(640, h)
        yb[p][:, :h] = dot(perm[1 if p == 2 else 0], got).astype(BF16)
        return block

    step = 512

    def terms(s, axes, out):
        acc = jnp.zeros((320, step), F32)
        for p in axes:
            h = halves[s][p]
            for i in range(2):
                w = wv[out, starts[s][p] + i * h : starts[s][p] + (i + 1) * h]
                acc = acc + dot_t(yb[p][i * 320 : (i + 1) * 320, :h], w)
        return acc

    def back(unit_y, unit_z):
        first = number(unit_z, unit_y, 0, 0)
        here = pl.ds(pl.multiple_of((unit_y * 4 + unit_z) * 80, 80), 80)
        there = pl.ds(pl.multiple_of(first * CAP, 80), 80)
        row = iota((80, 1), 0)
        j = rem(row, 10)
        lanes = iota((80, 128), 1)
        spread = jnp.where(iota((80, 8), 1) == div(row, 10), 1.0, 0.0)
        weights = dot(spread.astype(BF16), cwr[pl.ds(unit_y * 8, 8)].reshape(8, 128).astype(BF16))
        weight = jnp.sum(jnp.where(lanes == unit_z * CAP + j, weights, 0.0), axis=1, keepdims=True)
        total = raw[here, :]
        summed = jnp.sum(hs[there, :].astype(F32) * total, axis=1, keepdims=True)
        hs[there, :] = (weight * total).astype(BF16)
        pltpu.make_async_copy(hs.at[there], out_ref.at[0, there], l_out.at[unit_y * 4 + unit_z]).start()
        cells = jnp.where(lanes == j, summed, 0.0)
        for g in range(8):
            line = jnp.sum(cells[g * 10 : g * 10 + 10, :], axis=0, keepdims=True)
            sbs[first + g] = line

            @pl.when(first + g == me)
            def _():
                sbr[me] = line

            @pl.when(first + g != me)
            def _():
                pltpu.make_async_remote_copy(
                    sbs.at[first + g], sbr.at[me], s_sb, r_sb,
                    device_id=place(unit_z, unit_y, g // 2, g % 2), device_id_type=MESH,
                ).start()

    def receive_stage(s, k):
        y_block = arrive(s, 0, k)
        arrive(s, 2, k)
        here = pl.ds(pl.multiple_of(y_block * 320, 320), 320)

        def multiply(n, _):
            out = pl.ds(pl.multiple_of(n * step, step), step)
            raw[here, out] += terms(s, (0, 2), out)
            return 0

        lax.fori_loop(0, ff // step, multiply, 0)
        z_block = arrive(s, 1, k)

        def multiply_y(n, _):
            out = pl.ds(pl.multiple_of(n * step, step), step)
            acc = terms(s, (1,), out)
            for b in range(4):
                rows_b = pl.ds(pl.multiple_of(b * 320 + z_block * 80, 80), 80)
                raw[rows_b, out] += acc[b * 80 : (b + 1) * 80]
            return 0

        lax.fori_loop(0, ff // step, multiply_y, 0)
        if s < SETS[-1]:
            return

        def finish(i, _):
            back(y_block, (z + 4 - (i + 1) % 4) % 4)
            return 0

        lax.fori_loop(0, k + 1, finish, 0)

        def finish_z(i, _):
            back((y + 4 - (i + 1) % 4) % 4, z_block)
            return 0

        lax.fori_loop(0, k, finish_z, 0)

    def loop(lower, upper, *steps):
        def run(k, _):
            for do in steps:
                do(k)
            return 0

        lax.fori_loop(lower, upper, run, 0)

    def send_cw(i):
        unit_y, g = (y + i // 8) % 4, (x * 2 + c + i) % 8
        return pltpu.make_async_remote_copy(
            cws.at[unit_y * 8 + g], cwr.at[slot[0]], s_cw, r_cw,
            device_id=place(z, unit_y, g // 2, g % 2), device_id_type=MESH,
        )

    relay(0)
    stages = 4 * len(SETS)
    behind = 2

    def turn(t, _):
        for s in SETS:

            @pl.when(t == s * 4)
            def _():
                arrived(s)

            @pl.when(t // 4 == s)
            def _():
                send_stage(s, t % 4)

            if s > 0:

                @pl.when(t == s - 1)
                def _():
                    relay(s)

        @pl.when(t == behind - 1)
        def _():
            loop(1, 32, lambda i: send_cw(i).start())
            cwr[slot[0]] = cws[slot[0]]
            load_w.wait()
            load_hs.wait()

        u = t - behind
        for s in SETS:
            if s == SETS[-1]:

                @pl.when(u == s * 4)
                def _():
                    pltpu.make_async_copy(all_cw, all_cw, r_cw).wait()

            @pl.when((u >= s * 4) & (u < s * 4 + 4))
            def _():
                sent(s, u - s * 4)
                receive_stage(s, u - s * 4)
        return 0

    all_cw = cwr.at[pl.ds(0, 31)]
    lax.fori_loop(0, stages + behind, turn, 0)

    all_sb = sbr.at[pl.ds(0, 127)]
    pltpu.make_async_copy(all_sb, all_sb, r_sb).wait()
    returned = sbr[...].reshape(128, 128)
    mine = zpos[z]
    found = jnp.zeros((128, 128), F32)
    for j in range(CAP):
        found = found + jnp.where(mine == float(j), returned[:, j : j + 1], 0.0)
    for k in range(8):
        chosen = jnp.where(expert == ids[z, k : k + 1, :], found, 0.0)
        comb_ref[k : k + 1, :] = jnp.sum(chosen, axis=0, keepdims=True)

    for s in SETS:
        for p in AXES:
            for d in (1, 3):
                gather(s, p, d).wait_send()
                forward(s, p, d).wait_send()
    pltpu.make_async_copy(nine, nine, s_id).wait()
    pltpu.make_async_copy(all_cw, all_cw, s_cw).wait()
    pltpu.make_async_copy(all_sb, all_sb, s_sb).wait()

    def stored(u):
        pltpu.make_async_copy(hs.at[pl.ds(0, 80)], out_ref.at[0, pl.ds(0, 80)], l_out.at[u]).wait()

    loop(0, 16, stored)


def per_device(out_grad, combine_weights, expert_ids, hidden_saved, down_weight):
    slots, ff = hidden_saved.shape[1:]
    halves = tuple(tuple(128 * n for n in share) for share in SHARES)
    starts, at = [], 0
    for s in SETS:
        starts.append([])
        for p in AXES:
            starts[s].append(at)
            at += 2 * halves[s][p]
    anywhere = pl.BlockSpec(memory_space=pl.ANY)
    vmem = pl.BlockSpec(memory_space=pltpu.VMEM)
    dma = pltpu.SemaphoreType.DMA
    flat = [h for s in SETS for h in halves[s]]

    def body(*refs):
        kernel(halves, starts, ff, *refs)

    hidden_grad, combine = pl.pallas_call(
        body,
        out_shape=(
            jax.ShapeDtypeStruct(hidden_saved.shape, BF16),
            jax.ShapeDtypeStruct((8, 128), F32),
        ),
        in_specs=[vmem, vmem, anywhere, anywhere, anywhere],
        out_specs=(anywhere, vmem),
        scratch_shapes=[pltpu.VMEM((4, 128, 2 * h), BF16) for h in flat]
        + [pltpu.VMEM((32, 80, h), BF16) for h in flat] * 2
        + [pltpu.VMEM((640, max(halves[s][p] for s in SETS)), BF16) for p in AXES]
        + [
            pltpu.VMEM((12, 16, 128), F32),
            pltpu.VMEM((3, 128, 512), BF16),
            pltpu.VMEM((4, 128, 128), F32),
            pltpu.VMEM((2, 640, 640), BF16),
            pltpu.VMEM((ff, out_grad.shape[1]), BF16),
            pltpu.VMEM((slots, ff), F32),
            pltpu.VMEM((slots, ff), BF16),
            pltpu.VMEM((32, 1, 128), F32),
            pltpu.VMEM((32, 1, 128), F32),
            pltpu.VMEM((128, 1, 128), F32),
            pltpu.VMEM((128, 1, 128), F32),
        ]
        + [dma((9, 4))] * 2
        + [dma] * 2
        + [dma((3, 12))] * 2
        + [dma] * 6
        + [dma((16,)), dma((9,))],
        compiler_params=pltpu.CompilerParams(
            collective_id=0, has_side_effects=True, vmem_limit_bytes=62 << 20
        ),
    )(expert_ids.T, combine_weights.T, out_grad, hidden_saved, down_weight)
    return hidden_grad, combine.T


def solution(mesh):
    both = ("ctx", "tp")
    in_specs = (P(both, None), P(both, None), P(both, None), P(both, None, None), P(both, None, None))
    out_specs = (P(both, None, None), P(both, None))
    return jax.shard_map(
        per_device, mesh=mesh, in_specs=in_specs, out_specs=out_specs, check_vma=False
    )
```

time: 180 us -> 152 us (0.84)
  Pallas kernels: 173 us -> 147 us
  other arithmetic: 1.98 us -> 0 us
    pallas_call x1, Pallas kernels: 173 us -> 147 us  [per_device(): pl.pallas_call(body, out_shape=(jax.ShapeDtypeStruct(hidden_saved.shape,...]
where the time goes in v2:
time: 152 us
  Pallas kernels  147 us (97%)
  local copies, waits for them, and re-layouts  4.89 us (3%)
    pallas_call x1, Pallas kernels, per_device(): pl.pallas_call(body, out_shape=(jax.ShapeDtypeStruct(hidden_saved.shape,...  147 us
    unnamed x4, local copies, waits for them, and re-layouts  4.89 us

profile of v2, /device:TPU:1, one launch (start us, length us, event | category | flops | bytes accessed | tf_op | source)
XLA Modules:
  0.0 152.1 jit_solution(17094872011530254064)
XLA Ops:
  0.6 146.6 %shard_map.68 = (bf16[1,1280,1536]{2,1,0:T(8,128)(2,1)}, f32[8,128]{1,0:T(8,128)}) custom-call(s32[8,128]{1,0:T(8,128)} %bitcast.3, bf16[8,128]{1,0:T(8,128)(2,1)} %bitcast.5, bf16[128,4096]{1,0:T(8,128)(2,1)} %refs_2_.1, bf16[1,1280,1536]{2,1,0:T(8,128)(2,1)} %refs_3_.1, bf16[1,1536,4096]{2,1,0:T(8,128)(2,1)} %refs_4_.1), custom_call_target="tpu_custom_call" | custom-call | tf_op jit(solution)/shard_map/pallas_call | solution.py:443
  147.2 0.0 copy-start
  147.2 4.3 %copy.9 = bf16[1,1280,1536]{2,1,0:T(8,128)(2,1)} copy(bf16[1,1280,1536]{2,1,0:T(8,128)(2,1)} %get-tuple-element.8) | data formatting | bytes 7864320
  151.5 0.0 copy-done
  151.5 0.6 copy.10
Async XLA Ops:
  147.2 4.3 %copy-start = (f32[8,128]{1,0:T(8,128)S(1)}, f32[8,128]{1,0:T(8,128)}, u32[]{:S(2)}) copy-start(f32[8,128]{1,0:T(8,128)} %get-tuple-element.5) | copy-start | bytes 12292

commit v3 on v2

--- a/solution.py
+++ b/solution.py
@@ -51,8 +51,7 @@
         return got
 
     ag, snd, rcv = ([take(3) for _ in SETS] for _ in range(3))
-    yb = take(3)
-    ids, pos, zpos, perm, wv, raw, hs, cws, cwr, sbs, sbr = take(11)
+    yb, ids, pos, zpos, perm, wv, raw, hs, cws, cwr, col, sbs, sbr = take(13)
     s_ag, r_ag, s_id, r_id, s_mv, r_mv, s_cw, r_cw, s_sb, r_sb, l_w, l_hs, l_out, l_own = take(14)
 
     ctx, tp = lax.axis_index("ctx"), lax.axis_index("tp")
@@ -117,16 +116,6 @@
                 gather(s, p, d).start()
     load_w.start()
     load_hs.start()
-
-    for q in range(2):
-        row = iota((640, 1), 0)
-        chunk, b, g, j = div(row, 320), rem(div(row, 80), 4), rem(div(row, 10), 8), rem(row, 10)
-        if q == 0:
-            source = g * 80 + chunk * 40 + b * 10 + j
-        else:
-            source = (b * 2 + rem(g, 2)) * 80 + chunk * 40 + div(g, 2) * 10 + j
-        perm[q] = jnp.where(iota((640, 640), 1) == source, 1.0, 0.0).astype(BF16)
-    raw[...] = jnp.zeros_like(raw)
 
     before = jnp.where(iota((128, 128), 0) < iota((128, 128), 1), 1.0, 0.0).astype(BF16)
     expert = iota((128, 128), 0).astype(F32)
@@ -165,7 +154,16 @@
             cws[unit_y * 8 + g] = rows[g : g + 1]
         return 0
 
-    lax.fori_loop(0, 4, weigh, 0)
+    def prepare():
+        for q in range(2):
+            row = iota((640, 1), 0)
+            chunk, b, g, j = div(row, 320), rem(div(row, 80), 4), rem(div(row, 10), 8), rem(row, 10)
+            if q == 0:
+                source = g * 80 + chunk * 40 + b * 10 + j
+            else:
+                source = (b * 2 + rem(g, 2)) * 80 + chunk * 40 + div(g, 2) * 10 + j
+            perm[q] = jnp.where(iota((640, 640), 1) == source, 1.0, 0.0).astype(BF16)
+        raw[...] = jnp.zeros_like(raw)
 
     def relay(s):
         for d in (1, 3):
@@ -216,12 +214,12 @@
             both = [part[g * 40 : g * 40 + 40] for part in parts]
             snd[s][p][k * 8 + g] = jnp.concatenate(both, axis=0).astype(BF16)
 
-    def send_stage(s, k):
-        for p in AXES:
+    def send_stage(s, k, axes=AXES):
+        for p in axes:
             pick(s, k, p)
 
         def send(i, _):
-            for p in AXES:
+            for p in axes:
                 own_g = (z if p == 2 else x) * 2 + c
                 g = (((z if p == 2 else x) + i + 1 + k) % 4) * 2 + (c + i // 4) % 2
                 itself = (k == 3) & (g == own_g)
@@ -256,53 +254,80 @@
         pltpu.make_async_copy(rows, rows, r_mv.at[s, p * 4 + block]).wait()
         h = halves[s][p]
         got = rcv[s][p][pl.ds(block * 8, 8)].reshape(640, h)
-        yb[p][:, :h] = dot(perm[1 if p == 2 else 0], got).astype(BF16)
+        ordered = dot(perm[1 if p == 2 else 0], got).astype(BF16)
+        off = 2 * halves[s][0] if p == 2 else 0
+        yb[:, off : off + h] = ordered[:320]
+        yb[:, off + h : off + 2 * h] = ordered[320:]
         return block
 
     step = 512
 
     def terms(s, axes, out):
-        acc = jnp.zeros((320, step), F32)
-        for p in axes:
-            h = halves[s][p]
-            for i in range(2):
-                w = wv[out, starts[s][p] + i * h : starts[s][p] + (i + 1) * h]
-                acc = acc + dot_t(yb[p][i * 320 : (i + 1) * 320, :h], w)
-        return acc
-
-    def back(unit_y, unit_z):
-        first = number(unit_z, unit_y, 0, 0)
-        here = pl.ds(pl.multiple_of((unit_y * 4 + unit_z) * 80, 80), 80)
-        there = pl.ds(pl.multiple_of(first * CAP, 80), 80)
+        start, width = starts[s][axes[0]], sum(2 * halves[s][p] for p in axes)
+        return dot_t(yb[:, :width], wv[out, start : start + width])
+
+    def column(unit_y, _):
         row = iota((80, 1), 0)
-        j = rem(row, 10)
-        lanes = iota((80, 128), 1)
         spread = jnp.where(iota((80, 8), 1) == div(row, 10), 1.0, 0.0)
         weights = dot(spread.astype(BF16), cwr[pl.ds(unit_y * 8, 8)].reshape(8, 128).astype(BF16))
-        weight = jnp.sum(jnp.where(lanes == unit_z * CAP + j, weights, 0.0), axis=1, keepdims=True)
-        total = raw[here, :]
-        summed = jnp.sum(hs[there, :].astype(F32) * total, axis=1, keepdims=True)
-        hs[there, :] = (weight * total).astype(BF16)
-        pltpu.make_async_copy(hs.at[there], out_ref.at[0, there], l_out.at[unit_y * 4 + unit_z]).start()
-        cells = jnp.where(lanes == j, summed, 0.0)
-        for g in range(8):
-            line = jnp.sum(cells[g * 10 : g * 10 + 10, :], axis=0, keepdims=True)
-            sbs[first + g] = line
-
-            @pl.when(first + g == me)
-            def _():
-                sbr[me] = line
-
-            @pl.when(first + g != me)
+        for unit_z in range(4):
+            mine = iota((80, 128), 1) == unit_z * CAP + rem(row, 10)
+            weight = jnp.sum(jnp.where(mine, weights, 0.0), axis=1, keepdims=True)
+            col[unit_y * 4 + unit_z] = jnp.broadcast_to(weight, (80, 128))
+        return 0
+
+    def finish(s, y_block):
+        here = pl.ds(pl.multiple_of(y_block * 320, 320), 320)
+        there = [pl.ds(pl.multiple_of((hi * 4 + y_block) * 160, 160), 160) for hi in range(2)]
+        weight = col[pl.ds(y_block * 4, 4)].reshape(320, 128)[:, :1]
+        summed = [jnp.zeros((160, 1), F32)] * 2
+        for n in range(ff // step):
+            out = slice(n * step, (n + 1) * step)
+            total = raw[here, out] + terms(s, (0, 2), out)
+            for hi in range(2):
+                part = total[hi * 160 : (hi + 1) * 160]
+                saved = hs[there[hi], out].astype(F32)
+                summed[hi] = summed[hi] + jnp.sum(saved * part, axis=1, keepdims=True)
+                hs[there[hi], out] = (weight[hi * 160 : (hi + 1) * 160] * part).astype(BF16)
+        for hi in range(2):
+            pltpu.make_async_copy(
+                hs.at[there[hi]], out_ref.at[0, there[hi]], l_out.at[y_block * 2 + hi]
+            ).start()
+        j = rem(iota((320, 1), 0), 10)
+        cells = jnp.where(iota((320, 128), 1) == j, jnp.concatenate(summed, axis=0), 0.0)
+        group = jnp.where(iota((32, 320), 0) == div(iota((1, 320), 1), 10), 1.0, 0.0).astype(BF16)
+        lines = jnp.zeros((32, 128), F32)
+        for _ in range(3):
+            piece = cells.astype(BF16)
+            lines = lines + dot(group, piece)
+            cells = cells - piece.astype(F32)
+        for i in range(32):
+            sbs[number(i // 8, y_block, 0, 0) + i % 8] = lines[i : i + 1]
+
+        def give(i, _):
+            who = number(i // 8, y_block, 0, 0) + i % 8
+
+            @pl.when(who == me)
+            def _():
+                sbr[me] = sbs[me]
+
+            @pl.when(who != me)
             def _():
                 pltpu.make_async_remote_copy(
-                    sbs.at[first + g], sbr.at[me], s_sb, r_sb,
-                    device_id=place(unit_z, unit_y, g // 2, g % 2), device_id_type=MESH,
+                    sbs.at[who], sbr.at[me], s_sb, r_sb,
+                    device_id=place(i // 8, y_block, (i // 2) % 4, i % 2), device_id_type=MESH,
                 ).start()
 
-    def receive_stage(s, k):
+            return 0
+
+        lax.fori_loop(0, 32, give, 0)
+
+    def receive_zx(s, k):
         y_block = arrive(s, 0, k)
         arrive(s, 2, k)
+        if s == SETS[-1]:
+            finish(s, y_block)
+            return
         here = pl.ds(pl.multiple_of(y_block * 320, 320), 320)
 
         def multiply(n, _):
@@ -311,9 +336,11 @@
             return 0
 
         lax.fori_loop(0, ff // step, multiply, 0)
+
+    def receive_y(s, k):
         z_block = arrive(s, 1, k)
 
-        def multiply_y(n, _):
+        def multiply(n, _):
             out = pl.ds(pl.multiple_of(n * step, step), step)
             acc = terms(s, (1,), out)
             for b in range(4):
@@ -321,21 +348,7 @@
                 raw[rows_b, out] += acc[b * 80 : (b + 1) * 80]
             return 0
 
-        lax.fori_loop(0, ff // step, multiply_y, 0)
-        if s < SETS[-1]:
-            return
-
-        def finish(i, _):
-            back(y_block, (z + 4 - (i + 1) % 4) % 4)
-            return 0
-
-        lax.fori_loop(0, k + 1, finish, 0)
-
-        def finish_z(i, _):
-            back((y + 4 - (i + 1) % 4) % 4, z_block)
-            return 0
-
-        lax.fori_loop(0, k, finish_z, 0)
+        lax.fori_loop(0, ff // step, multiply, 0)
 
     def loop(lower, upper, *steps):
         def run(k, _):
@@ -354,7 +367,7 @@
 
     relay(0)
     stages = 4 * len(SETS)
-    behind = 2
+    behind = 6
 
     def turn(t, _):
         for s in SETS:
@@ -365,7 +378,10 @@
 
             @pl.when(t // 4 == s)
             def _():
-                send_stage(s, t % 4)
+                if s < SETS[-1]:
+                    send_stage(s, t % 4)
+                else:
+                    send_stage(s, t % 4)
 
             if s > 0:
 
@@ -373,8 +389,10 @@
                 def _():
                     relay(s)
 
-        @pl.when(t == behind - 1)
+        @pl.when(t == 1)
         def _():
+            prepare()
+            lax.fori_loop(0, 4, weigh, 0)
             loop(1, 32, lambda i: send_cw(i).start())
             cwr[slot[0]] = cws[slot[0]]
             load_w.wait()
@@ -387,11 +405,22 @@
                 @pl.when(u == s * 4)
                 def _():
                     pltpu.make_async_copy(all_cw, all_cw, r_cw).wait()
+                    lax.fori_loop(0, 4, column, 0)
 
             @pl.when((u >= s * 4) & (u < s * 4 + 4))
             def _():
-                sent(s, u - s * 4)
-                receive_stage(s, u - s * 4)
+                k = u - s * 4
+                sent(s, k)
+                if s < SETS[-1]:
+                    receive_zx(s, k)
+                    receive_y(s, k)
+                else:
+
+                    @pl.when(k == 0)
+                    def _():
+                        loop(0, 4, lambda j: receive_y(s, j))
+
+                    receive_zx(s, k)
         return 0
 
     all_cw = cwr.at[pl.ds(0, 31)]
@@ -418,9 +447,9 @@
     pltpu.make_async_copy(all_sb, all_sb, s_sb).wait()
 
     def stored(u):
-        pltpu.make_async_copy(hs.at[pl.ds(0, 80)], out_ref.at[0, pl.ds(0, 80)], l_out.at[u]).wait()
-
-    loop(0, 16, stored)
+        pltpu.make_async_copy(hs.at[pl.ds(0, 160)], out_ref.at[0, pl.ds(0, 160)], l_out.at[u]).wait()
+
+    loop(0, 8, stored)
 
 
 def per_device(out_grad, combine_weights, expert_ids, hidden_saved, down_weight):
@@ -428,9 +457,9 @@
     halves = tuple(tuple(128 * n for n in share) for share in SHARES)
     starts, at = [], 0
     for s in SETS:
-        starts.append([])
-        for p in AXES:
-            starts[s].append(at)
+        starts.append([0, 0, 0])
+        for p in (0, 2, 1):
+            starts[s][p] = at
             at += 2 * halves[s][p]
     anywhere = pl.BlockSpec(memory_space=pl.ANY)
     vmem = pl.BlockSpec(memory_space=pltpu.VMEM)
@@ -450,7 +479,7 @@
         out_specs=(anywhere, vmem),
         scratch_shapes=[pltpu.VMEM((4, 128, 2 * h), BF16) for h in flat]
         + [pltpu.VMEM((32, 80, h), BF16) for h in flat] * 2
-        + [pltpu.VMEM((640, max(halves[s][p] for s in SETS)), BF16) for p in AXES]
+        + [pltpu.VMEM((320, max(2 * (halves[s][0] + halves[s][2]) for s in SETS)), BF16)]
         + [
             pltpu.VMEM((12, 16, 128), F32),
             pltpu.VMEM((3, 128, 512), BF16),
@@ -461,6 +490,7 @@
             pltpu.VMEM((slots, ff), BF16),
             pltpu.VMEM((32, 1, 128), F32),
             pltpu.VMEM((32, 1, 128), F32),
+            pltpu.VMEM((16, 80, 128), F32),
             pltpu.VMEM((128, 1, 128), F32),
             pltpu.VMEM((128, 1, 128), F32),
         ]
@@ -468,7 +498,7 @@
         + [dma] * 2
         + [dma((3, 12))] * 2
         + [dma] * 6
-        + [dma((16,)), dma((9,))],
+        + [dma((8,)), dma((9,))],
         compiler_params=pltpu.CompilerParams(
             collective_id=0, has_side_effects=True, vmem_limit_bytes=62 << 20
         ),

time: 152 us -> 139 us (0.914)
  Pallas kernels: 147 us -> 134 us
    pallas_call x1, Pallas kernels: 147 us -> 134 us  [per_device(): pl.pallas_call(body, out_shape=(jax.ShapeDtypeStruct(hidden_saved.shape,...]
where the time goes in v3:
time: 139 us
  Pallas kernels  134 us (96%)
  local copies, waits for them, and re-layouts  4.89 us (4%)
    pallas_call x1, Pallas kernels, per_device(): pl.pallas_call(body, out_shape=(jax.ShapeDtypeStruct(hidden_saved.shape,...  134 us
    unnamed x4, local copies, waits for them, and re-layouts  4.89 us

profile of v3, /device:TPU:1, one launch (start us, length us, event | category | flops | bytes accessed | tf_op | source)
XLA Modules:
  0.0 139.2 jit_solution(4681016580062011255)
XLA Ops:
  0.6 133.7 %shard_map.68 = (bf16[1,1280,1536]{2,1,0:T(8,128)(2,1)}, f32[8,128]{1,0:T(8,128)}) custom-call(s32[8,128]{1,0:T(8,128)} %bitcast.3, bf16[8,128]{1,0:T(8,128)(2,1)} %bitcast.5, bf16[128,4096]{1,0:T(8,128)(2,1)} %refs_2_.1, bf16[1,1280,1536]{2,1,0:T(8,128)(2,1)} %refs_3_.1, bf16[1,1536,4096]{2,1,0:T(8,128)(2,1)} %refs_4_.1), custom_call_target="tpu_custom_call" | custom-call | tf_op jit(solution)/shard_map/pallas_call | solution.py:472
  134.3 0.0 copy-start
  134.3 4.3 %copy.9 = bf16[1,1280,1536]{2,1,0:T(8,128)(2,1)} copy(bf16[1,1280,1536]{2,1,0:T(8,128)(2,1)} %get-tuple-element.8) | data formatting | bytes 7864320
  138.6 0.0 copy-done
  138.6 0.6 copy.10
Async XLA Ops:
  134.3 4.3 %copy-start = (f32[8,128]{1,0:T(8,128)S(1)}, f32[8,128]{1,0:T(8,128)}, u32[]{:S(2)}) copy-start(f32[8,128]{1,0:T(8,128)} %get-tuple-element.5) | copy-start | bytes 12292

commit v4 on v3

--- a/solution.py
+++ b/solution.py
@@ -260,7 +260,7 @@
         yb[:, off + h : off + 2 * h] = ordered[320:]
         return block
 
-    step = 512
+    step = 768
 
     def terms(s, axes, out):
         start, width = starts[s][axes[0]], sum(2 * halves[s][p] for p in axes)

time: 139 us -> 136 us (0.978)
  Pallas kernels: 134 us -> 131 us
    pallas_call x1, Pallas kernels: 134 us -> 131 us  [per_device(): pl.pallas_call(body, out_shape=(jax.ShapeDtypeStruct(hidden_saved.shape,...]
where the time goes in v4:
time: 136 us
  Pallas kernels  131 us (96%)
  local copies, waits for them, and re-layouts  4.89 us (4%)
    pallas_call x1, Pallas kernels, per_device(): pl.pallas_call(body, out_shape=(jax.ShapeDtypeStruct(hidden_saved.shape,...  131 us
    unnamed x4, local copies, waits for them, and re-layouts  4.89 us

profile of v4, /device:TPU:1, one launch (start us, length us, event | category | flops | bytes accessed | tf_op | source)
XLA Modules:
  0.0 136.0 jit_solution(16333812599752008555)
XLA Ops:
  0.6 130.5 %shard_map.68 = (bf16[1,1280,1536]{2,1,0:T(8,128)(2,1)}, f32[8,128]{1,0:T(8,128)}) custom-call(s32[8,128]{1,0:T(8,128)} %bitcast.3, bf16[8,128]{1,0:T(8,128)(2,1)} %bitcast.5, bf16[128,4096]{1,0:T(8,128)(2,1)} %refs_2_.1, bf16[1,1280,1536]{2,1,0:T(8,128)(2,1)} %refs_3_.1, bf16[1,1536,4096]{2,1,0:T(8,128)(2,1)} %refs_4_.1), custom_call_target="tpu_custom_call" | custom-call | tf_op jit(solution)/shard_map/pallas_call | solution.py:472
  131.1 0.0 copy-start
  131.1 4.3 %copy.9 = bf16[1,1280,1536]{2,1,0:T(8,128)(2,1)} copy(bf16[1,1280,1536]{2,1,0:T(8,128)(2,1)} %get-tuple-element.8) | data formatting | bytes 7864320
  135.4 0.0 copy-done
  135.4 0.6 copy.10
Async XLA Ops:
  131.1 4.3 %copy-start = (f32[8,128]{1,0:T(8,128)S(1)}, f32[8,128]{1,0:T(8,128)}, u32[]{:S(2)}) copy-start(f32[8,128]{1,0:T(8,128)} %get-tuple-element.5) | copy-start | bytes 12292
